TPU v7x, 256 devices: a whole 4x4x8 slice. The times are simulated.
256 devices in a mesh: band: 64 (over y, z, core), rep: 4 (over x).
Axes of the slice: x: 4, y: 4, z: 8, core: 2. Of those that a mesh axis runs over, the one named last changes fastest.
Arguments:
- embeddings: bfloat16 [128, 32768], P('rep', 'band'), may hold values from -6 to 6
- route: int32 [32768, 1], P('band'), may hold values from 0 to 63; in each aligned block of 512 rows (0 to 511, 512 to 1023, ...) at most 20 rows name the same one
- place: bfloat16 [2, 32768], P(None, 'band'), may hold values from 0 to 1
- scales: float32 [4], replicated, may hold values from 0.25 to 1
- first_weight: bfloat16 [512, 512], replicated, may hold values from -0.25 to 0.25
- first_bias: float32 [512], replicated, may hold values from -3 to 3
- second_weight: bfloat16 [512, 512], replicated, may hold values from -0.25 to 0.25
- out_cotangent: bfloat16 [512, 768, 256], P(None, ('band', 'rep')), may hold values from -6 to 6
Outputs:
- embed_gradient: float32 [128, 32768], P('rep', 'band')
- first_weight_gradient: float32 [512, 512], replicated
- first_bias_gradient: float32 [512], replicated
- second_weight_gradient: float32 [512, 512], replicated
Inputs may be any that keep to these rules, and one draw needn't show every extreme that they name: `route`: within the 512 reports of one feed (aligned blocks of rows), at most 20 name the same band, and in some block exactly 20 do.
All inputs are finite; a program needn't handle non-finite values.
Results may differ from a plain program's by a relative error of at most 0.0063.
Values may be sent and summed in bfloat16 or wider, within the bound.
A program may use at most 128 MiB of HBM per device.

v0:
```python
import jax
import jax.numpy as jnp
from jax import lax
from jax.sharding import PartitionSpec as P

root_two_pi = 0.7978845608028654
cubic = 0.044715


def gelu_value(value):
    inner = root_two_pi * (value + cubic * value * value * value)
    return 0.5 * value * (1.0 + jnp.tanh(inner))


def gelu_slope(value):
    tangent = jnp.tanh(root_two_pi * (value + cubic * value * value * value))
    return 0.5 * (1.0 + tangent) + 0.5 * value * (1.0 - tangent * tangent) * root_two_pi * (
        1.0 + 3.0 * cubic * value * value
    )


def kernel_factors(geometry, block, scales, lat_rows, columns):
    north_fraction = geometry[0]
    east_fraction = geometry[1]
    valid = geometry[2]
    centre_rows = jnp.arange(lat_rows, dtype=jnp.float32) + 0.5
    north_gap = (
        ((1 - block).astype(jnp.float32) * lat_rows)[None, :]
        + centre_rows[:, None]
        - (north_fraction * lat_rows)[None, :]
    )
    east_gap = (jnp.arange(columns, dtype=jnp.float32) + 0.5)[:, None] - (east_fraction * columns)[
        None, :
    ]
    reach = scales * lat_rows
    inverse = 0.5 / (reach * reach)
    row_kernel = (
        jnp.exp(-(north_gap * north_gap)[None] * inverse[:, None, None]) * valid[None, None, :]
    ).astype(jnp.bfloat16)
    column_kernel = jnp.exp(-(east_gap * east_gap)[None] * inverse[:, None, None]).astype(
        jnp.bfloat16
    )
    return (row_kernel, column_kernel)


def splat(embedded, row_kernel, column_kernel):
    channels = embedded.shape[0]
    levels, lat_rows, slots = row_kernel.shape
    columns = column_kernel.shape[1]
    sums = []
    weights = []
    for level in range(levels):
        weighted = (embedded[:, None, :] * row_kernel[level][None]).reshape(
            channels * lat_rows, slots
        )
        sums.append(
            lax.dot_general(
                weighted,
                column_kernel[level],
                (((1,), (1,)), ((), ())),
                preferred_element_type=jnp.float32,
            )
        )
        weights.append(
            lax.dot_general(
                row_kernel[level],
                column_kernel[level],
                (((1,), (1,)), ((), ())),
                preferred_element_type=jnp.float32,
            )
        )
    splatted = jnp.stack(sums).reshape(levels, channels, lat_rows * columns)
    density = jnp.stack(weights).reshape(levels, lat_rows * columns)
    features = (
        (splatted / (density[:, None, :] + 1.0))
        .transpose(1, 0, 2)
        .reshape(channels * levels, lat_rows * columns)
        .astype(jnp.bfloat16)
    )
    return (features, density)


def spread_back(gradient, row_kernel, column_kernel):
    levels, lat_rows, slots = row_kernel.shape
    columns = column_kernel.shape[1]
    channels = gradient.shape[0] // levels
    grid = gradient.reshape(channels, levels, lat_rows * columns)
    total = jnp.zeros((channels, slots), jnp.float32)
    for level in range(levels):
        slab = grid[:, level].reshape(channels * lat_rows, columns)
        along = jnp.dot(slab, column_kernel[level], preferred_element_type=jnp.float32).reshape(
            channels, lat_rows, slots
        )
        total = total + jnp.sum(along * row_kernel[level][None].astype(jnp.float32), axis=1)
    return total


def band_ranks(route_rows, bands):
    owner = route_rows[:, 0]
    onehot = (owner[:, None] == jnp.arange(bands, dtype=jnp.int32)[None, :]).astype(jnp.int32)
    running = jnp.cumsum(onehot, axis=0)
    return (owner, jnp.sum((running - 1) * onehot, axis=1))


def on_device(
    embeddings, route, place, scales, first_weight, first_bias, second_weight, out_cotangent
):
    channels, reports = embeddings.shape
    bands = lax.axis_size("band")
    parts = lax.axis_size("rep")
    quarter = lax.axis_index("rep")
    capacity = max(2, 5 * reports // (2 * bands))
    sub_rows = out_cotangent.shape[1]
    lat_rows = sub_rows * parts
    columns = out_cotangent.shape[2]
    levels = scales.shape[0]
    owner, rank = band_ranks(route, bands)
    packed = jnp.concatenate([embeddings, place, jnp.ones((1, reports), jnp.bfloat16)], axis=0)
    rows = channels + 3
    span = 3 * capacity
    outgoing = jnp.zeros((rows, bands * span), jnp.bfloat16)
    for offset in range(3):
        target = owner + 1 - offset
        inside = (target >= 0) & (target < bands)
        where_to = jnp.where(inside, target * span + offset * capacity + rank, bands * span)
        outgoing = outgoing.at[:, where_to].set(packed, mode="drop")
    nearby = lax.all_to_all(outgoing, "band", split_axis=1, concat_axis=1, tiled=True)
    block = jnp.arange(bands * span, dtype=jnp.int32) // capacity % 3
    geometry = nearby[channels:].astype(jnp.float32)
    row_kernel, column_kernel = kernel_factors(geometry, block, scales, lat_rows, columns)
    features, density = splat(nearby[:channels], row_kernel, column_kernel)
    cotangent = out_cotangent.reshape(out_cotangent.shape[0], sub_rows * columns)
    mine = lax.all_to_all(features, "rep", split_axis=1, concat_axis=0, tiled=True)
    local_density = lax.dynamic_slice_in_dim(
        density.reshape(levels, lat_rows, columns), quarter * sub_rows, sub_rows, 1
    ).reshape(levels, sub_rows * columns)
    preact = (
        lax.dot_general(
            first_weight, mine, (((0,), (0,)), ((), ())), preferred_element_type=jnp.float32
        )
        + first_bias[:, None]
    )
    hidden = gelu_value(preact).astype(jnp.bfloat16)
    pre_gradient = (
        jnp.dot(second_weight, cotangent, preferred_element_type=jnp.float32) * gelu_slope(preact)
    ).astype(jnp.bfloat16)
    first_sum = lax.dot_general(
        mine, pre_gradient, (((1,), (1,)), ((), ())), preferred_element_type=jnp.float32
    )
    second_sum = lax.dot_general(
        hidden, cotangent, (((1,), (1,)), ((), ())), preferred_element_type=jnp.float32
    )
    bias_sum = jnp.sum(pre_gradient.astype(jnp.float32), axis=1)
    feature_gradient = jnp.dot(first_weight, pre_gradient, preferred_element_type=jnp.float32)
    count = sub_rows * columns
    cell_part = (
        (feature_gradient.reshape(-1, levels, count) / (local_density[None] + 1.0))
        .reshape(-1, count)
        .astype(jnp.bfloat16)
    )
    splat_gradient = lax.all_to_all(cell_part, "rep", split_axis=0, concat_axis=1, tiled=True)
    totals = lax.psum((first_sum, second_sum, bias_sum), ("band", "rep"))
    slot_gradient = spread_back(splat_gradient, row_kernel, column_kernel)
    backward = lax.all_to_all(slot_gradient, "band", split_axis=1, concat_axis=1, tiled=True)
    embed_gradient = jnp.zeros((channels, reports), jnp.float32)
    for offset in range(3):
        target = owner + 1 - offset
        inside = (target >= 0) & (target < bands)
        where_from = jnp.where(inside, target * span + offset * capacity + rank, 0)
        embed_gradient = embed_gradient + jnp.where(inside[None, :], backward[:, where_from], 0.0)
    return (embed_gradient, totals[0], totals[2], totals[1])


def solution(mesh):
    return jax.shard_map(
        on_device,
        mesh=mesh,
        in_specs=(
            P("rep", "band"),
            P("band", None),
            P(None, "band"),
            P(),
            P(),
            P(),
            P(),
            P(None, ("band", "rep"), None),
        ),
        out_specs=(P("rep", "band"), P(), P(), P()),
        check_vma=False,
    )
```

profile of v0, /device:TPU:2, one launch (start us, length us, event | category | flops | bytes accessed | tf_op | source)
XLA Modules:
  0.0 443.6 jit_solution(7938262040771985791)
XLA Ops:
  14.1 2.3 scatter_fusion
  16.5 2.3 scatter_fusion.1
  21.7 12.3 %all-to-all-start = ((bf16[64,2,1050]{2,1,0:T(2,128)(2,1)}), bf16[64,2,1050]{2,1,0:T(2,128)(2,1)S(1)}, u32[]{:S(2)}, u32[]{:S(2)}) async-start(bf16[64,2,1050]{2,1,0:T(2,128)(2,1)} %reshape.419), calls=%async_computation | async-start | bytes 589824 | tf_op jit(solution)/shard_map/all_to_all | solution.py:127
  34.1 12.5 %all-to-all-done = bf16[64,2,1050]{2,1,0:T(2,128)(2,1)S(1)} async-done(((bf16[64,2,1050]{2,1,0:T(2,128)(2,1)}), bf16[64,2,1050]{2,1,0:T(2,128)(2,1)S(1)}, u32[]{:S(2)}, u32[]{:S(2)}) %all-to-all-start) | async-done | bytes 268832 | tf_op jit(solution)/shard_map/all_to_all | solution.py:127
  50.7 2.9 exponential_convert_fusion
  58.4 6.8 %broadcast_multiply_fusion.3 = (bf16[32,12,3840]{2,1,0:T(8,128)(2,1)}, bf16[32,12,3840]{2,1,0:T(8,128)(2,1)}, bf16[32,12,3840]{2,1,0:T(8,128)(2,1)}, bf16[32,12,3840]{2,1,0:T(8,128)(2,1)}) fusion(bf16[12,3840]{1,0:T(8,128)(2,1)} %get-tuple-element.32, bf16[32,3840]{1,0:T(8,128)(2,1)S(1)} %mul.298, bf16[12,3840]{1,0:T(8,128)(2,1)} %get-tuple-element.31, ...), kind=kLoop, calls=%fused_computation.37 | loop fusion | flops 5898240 | bytes 12410880 | tf_op jit(solution)/shard_map/mul | solution.py:53
  65.2 3.9 mul.315
  69.1 3.2 fusion.18
  72.3 2.1 stack.55
  74.5 3.9 mul.326
  78.4 3.3 fusion.14
  81.6 2.2 stack.56
  83.8 3.9 mul.330
  87.7 3.2 fusion.10
  90.9 2.1 stack.57
  93.1 4.1 mul.334
  97.2 3.2 fusion.6
  102.0 2.8 fusion.54
  106.0 4.8 %all-to-all-start.1 = ((bf16[128,4,768]{2,0,1:T(8,128)(2,1)}), bf16[128,4,768]{2,0,1:T(8,128)(2,1)S(1)}, u32[]{:S(2)}, u32[]{:S(2)}) async-start(bf16[128,4,768]{2,0,1:T(8,128)(2,1)} %copy.51), calls=%async_computation.1 | async-start | bytes 1572864 | tf_op jit(solution)/shard_map/all_to_all | solution.py:133
  114.0 7.9 %all-to-all-done.1 = bf16[128,4,768]{2,0,1:T(8,128)(2,1)S(1)} async-done(((bf16[128,4,768]{2,0,1:T(8,128)(2,1)}), bf16[128,4,768]{2,0,1:T(8,128)(2,1)S(1)}, u32[]{:S(2)}, u32[]{:S(2)}) %all-to-all-start.1) | async-done | bytes 786464 | tf_op jit(solution)/shard_map/all_to_all | solution.py:133
  126.0 5.3 %all-to-all-start.2 = ((bf16[4,128,768]{2,1,0:T(8,128)(2,1)}), bf16[4,128,768]{2,1,0:T(8,128)(2,1)S(1)}, u32[]{:S(2)}, u32[]{:S(2)}) async-start(bf16[4,128,768]{2,1,0:T(8,128)(2,1)} %bitcast.182), calls=%async_computation.2 | async-start | bytes 1572864 | tf_op jit(solution)/shard_map/all_to_all | solution.py:161
  131.4 3.0 fusion.53
  134.4 6.8 %all-to-all-done.2 = bf16[4,128,768]{2,1,0:T(8,128)(2,1)S(1)} async-done(((bf16[4,128,768]{2,1,0:T(8,128)(2,1)}), bf16[4,128,768]{2,1,0:T(8,128)(2,1)S(1)}, u32[]{:S(2)}, u32[]{:S(2)}) %all-to-all-start.2) | async-done | bytes 786464 | tf_op jit(solution)/shard_map/all_to_all | solution.py:161
  142.1 3.4 slice_reduce_fusion.2
  145.6 2.7 fusion.23
  148.3 2.6 fusion.20
  155.2 2.6 reshape.421
  157.8 5.9 %all-to-all-start.3 = ((f32[64,1,1920]{2,1,0:T(1,128)}), f32[64,1,1920]{2,1,0:T(1,128)S(1)}, u32[]{:S(2)}, u32[]{:S(2)}) async-start(f32[64,1,1920]{2,1,0:T(1,128)} %reshape.421), calls=%async_computation.3 | async-start | bytes 983040 | tf_op jit(solution)/shard_map/all_to_all | solution.py:164
  163.8 2.7 fusion.90
  166.6 77.1 %psum.22 = f32[512]{0:T(512)} all-reduce(f32[512]{0:T(512)S(1)} %get-tuple-element.46), channel_id=1, replica_groups=mesh['band'=64,'rep'=4] {'band','rep'}, use_global_device_ids=true, to_apply=%region_12.13 | all-reduce | flops 512 | bytes 4096 | tf_op jit(solution)/shard_map/psum | solution.py:162
  253.5 179.7 %all-reduce.3.cloned.1.call-done = (f32[512,512]{1,0:T(8,128)}, f32[512,512]{1,0:T(8,128)}) async-done(((f32[512,512]{1,0:T(8,128)}, f32[512,512]{1,0:T(8,128)}), (f32[512,512]{1,0:T(8,128)}, f32[512,512]{1,0:T(8,128)})) %all-reduce.3.cloned.1.call-update) | async-done | bytes 2097168 | tf_op jit(solution)/shard_map/psum | solution.py:162
  433.2 2.4 copy.100
  (116 shorter events, 44.6 us)
Async XLA Ops:
  7.2 114.8 %copy-start = (bf16[512,512]{1,0:T(8,128)(2,1)S(1)}, bf16[512,512]{1,0:T(8,128)(2,1)}, u32[]{:S(2)}) copy-start(bf16[512,512]{1,0:T(8,128)(2,1)} %param.12) | copy-start | bytes 1572868
  19.1 15.0 %copy-start.15 = (f32[4]{0:T(128)S(1)}, f32[4]{0:T(128)}, u32[]{:S(2)}) copy-start(f32[4]{0:T(128)} %param.11) | copy-start | bytes 52
  21.7 24.9 %all-to-all-start = ((bf16[64,2,1050]{2,1,0:T(2,128)(2,1)}), bf16[64,2,1050]{2,1,0:T(2,128)(2,1)S(1)}, u32[]{:S(2)}, u32[]{:S(2)}) async-start(bf16[64,2,1050]{2,1,0:T(2,128)(2,1)} %reshape.419), calls=%async_computation | async-start | bytes 589824 | tf_op jit(solution)/shard_map/all_to_all | solution.py:127
  48.3 0.8 copy-start.2
  53.6 3.1 copy-start.1
  53.7 1.7 copy-start.3
  105.0 5.8 %copy-start.6 = (bf16[512,3,256]{2,0,1:T(8,128)(2,1)S(1)}, bf16[512,3,256]{2,0,1:T(8,128)(2,1)}, u32[]{:S(2)}) copy-start(bf16[512,3,256]{2,0,1:T(8,128)(2,1)} %param.15) | copy-start | bytes 2359300
  106.0 15.9 %all-to-all-start.1 = ((bf16[128,4,768]{2,0,1:T(8,128)(2,1)}), bf16[128,4,768]{2,0,1:T(8,128)(2,1)S(1)}, u32[]{:S(2)}, u32[]{:S(2)}) async-start(bf16[128,4,768]{2,0,1:T(8,128)(2,1)} %copy.51), calls=%async_computation.1 | async-start | bytes 1572864 | tf_op jit(solution)/shard_map/all_to_all | solution.py:133
  112.2 9.7 %copy-start.14 = (f32[512]{0:T(512)S(1)}, f32[512]{0:T(512)}, u32[]{:S(2)}) copy-start(f32[512]{0:T(512)} %param.13) | copy-start | bytes 6148
  114.0 8.6 %copy-start.7 = (bf16[512,3,256]{0,2,1:T(8,128)(2,1)S(1)}, bf16[512,3,256]{0,2,1:T(8,128)(2,1)}, u32[]{:S(2)}) copy-start(bf16[512,3,256]{0,2,1:T(8,128)(2,1)} %copy.39) | copy-start | bytes 2359300
  114.0 8.6 %copy-start.13 = (bf16[512,512]{1,0:T(8,128)(2,1)S(1)}, bf16[512,512]{1,0:T(8,128)(2,1)}, u32[]{:S(2)}) copy-start(bf16[512,512]{1,0:T(8,128)(2,1)} %param.14) | copy-start | bytes 1572868
  122.6 1.4 copy-start.16
  122.6 2.0 copy-start.4
  123.9 2.1 copy-start.8
  126.0 15.2 %all-to-all-start.2 = ((bf16[4,128,768]{2,1,0:T(8,128)(2,1)}), bf16[4,128,768]{2,1,0:T(8,128)(2,1)S(1)}, u32[]{:S(2)}, u32[]{:S(2)}) async-start(bf16[4,128,768]{2,1,0:T(8,128)(2,1)} %bitcast.182), calls=%async_computation.2 | async-start | bytes 1572864 | tf_op jit(solution)/shard_map/all_to_all | solution.py:161
  142.1 8.7 %slice-start = ((s8[7864320]{0:T(1024)(128)(4,1)}), s8[3670016]{0:T(1024)(128)(4,1)S(1)}, s32[]{:S(2)}) async-start(s8[7864320]{0:T(1024)(128)(4,1)} %bitcast.170), calls=%async_computation.5 | async-start | bytes 7340032
  145.5 2.7 copy-start.11
  145.5 5.3 %slice-start.1 = ((s8[7864320]{0:T(1024)(128)(4,1)}), s8[4194304]{0:T(1024)(128)(4,1)S(1)}, s32[]{:S(2)}) async-start(s8[7864320]{0:T(1024)(128)(4,1)} %bitcast.170), calls=%async_computation.6 | async-start | bytes 8388608
  148.2 2.6 copy-start.10
  150.9 1.0 copy-start.9
  157.8 85.9 %all-to-all-start.3 = ((f32[64,1,1920]{2,1,0:T(1,128)}), f32[64,1,1920]{2,1,0:T(1,128)S(1)}, u32[]{:S(2)}, u32[]{:S(2)}) async-start(f32[64,1,1920]{2,1,0:T(1,128)} %reshape.421), calls=%async_computation.3 | async-start | bytes 983040 | tf_op jit(solution)/shard_map/all_to_all | solution.py:164
  163.7 2.8 copy-start.12
  163.7 269.5 %all-reduce.3.cloned.1.call-start = ((), (), s32[]{:S(2)}) async-start(), calls=%async_computation.4 | async-start | bytes 4194304 | tf_op jit(solution)/shard_map/psum | solution.py:162
  433.2 2.4 copy-start.5
Sparse Core Ops, SparseCore 0:
  170.7 262.4 all-reduce.2
where the time goes:
time: 451 us; the launch traced here: 444 us
  waiting for transfers between devices  207 us (46%)
  blocking collectives  77.1 us (17%)
  local copies, waits for them, and re-layouts  61.9 us (14%)
  matrix products  32.9 us (7%)
  starting transfers between devices  28.4 us (6%)
  other arithmetic  21.3 us (5%)
  between operations  14.9 us (3%)
    psum x1, waiting for transfers between devices, on_device(): totals = lax.psum((first_sum, second_sum, bias_sum), ('band', 'rep'))  180 us
    psum x1, blocking collectives, on_device(): totals = lax.psum((first_sum, second_sum, bias_sum), ('band', 'rep'))  77.1 us
    mul x5, local copies, waits for them, and re-layouts, splat(): embedded[:, None, :] * row_kernel[level][None]  16.6 us
    unnamed x51, local copies, waits for them, and re-layouts  13.7 us
    dot_general x4, matrix products, splat(): lax.dot_general(weighted, column_kernel[level], (((1,), (1,)), ((), ())),...  13 us
    all_to_all x1, waiting for transfers between devices, on_device(): lax.all_to_all(outgoing, 'band', split_axis=1, concat_axis=1, tiled=True)  12.5 us
    all_to_all x1, starting transfers between devices, on_device(): lax.all_to_all(outgoing, 'band', split_axis=1, concat_axis=1, tiled=True)  12.3 us
  transfers between devices with their start and end apart: 5, of which 4 were waited for; matrix products, arithmetic and copies ran while one was open for 4% of the time, Pallas kernels for 0%

commit v1 on v0

--- a/solution.py
+++ b/solution.py
@@ -159,7 +159,7 @@
         .astype(jnp.bfloat16)
     )
     splat_gradient = lax.all_to_all(cell_part, "rep", split_axis=0, concat_axis=1, tiled=True)
-    totals = lax.psum((first_sum, second_sum, bias_sum), ("band", "rep"))
+    totals = lax.psum(lax.psum((first_sum, second_sum, bias_sum), "rep"), "band")
     slot_gradient = spread_back(splat_gradient, row_kernel, column_kernel)
     backward = lax.all_to_all(slot_gradient, "band", split_axis=1, concat_axis=1, tiled=True)
     embed_gradient = jnp.zeros((channels, reports), jnp.float32)

time: 451 us -> 408 us (0.905)
  waiting for transfers between devices: 207 us -> 105 us
  blocking collectives: 77.1 us -> 137 us
    psum x1 -> x2, waiting for transfers between devices: 180 us -> 79.3 us  [the longest x1 47.8 us: on_device(): lax.psum(lax.psum((first_sum, second_sum, bias_sum), 'rep'), 'band')]
    psum x1 -> x2, blocking collectives: 77.1 us -> 137 us  [the longest x1 128 us: on_device(): lax.psum(lax.psum((first_sum, second_sum, bias_sum), 'rep'), 'band')]
    unnamed x51 -> x55, local copies, waits for them, and re-layouts: 13.7 us -> 13.7 us
  transfers between devices with their start and end apart: 5 -> 6, of which waited for: 4 -> 5; matrix products, arithmetic and copies ran while one was open for 4% -> 8% of each run, Pallas kernels for 0% -> 0%
where the time goes in v1:
time: 408 us; the launch traced here: 401 us
  blocking collectives  137 us (34%)
  waiting for transfers between devices  105 us (26%)
  local copies, waits for them, and re-layouts  61.9 us (15%)
  matrix products  31.7 us (8%)
  starting transfers between devices  28.7 us (7%)
  other arithmetic  21.3 us (5%)
  between operations  14.9 us (4%)
    psum x1, blocking collectives, on_device(): lax.psum(lax.psum((first_sum, second_sum, bias_sum), 'rep'), 'band')  128 us
    psum x1, waiting for transfers between devices, on_device(): lax.psum(lax.psum((first_sum, second_sum, bias_sum), 'rep'), 'band')  47.8 us
    psum x1, waiting for transfers between devices, on_device(): lax.psum((first_sum, second_sum, bias_sum), 'rep')  31.5 us
    mul x5, local copies, waits for them, and re-layouts, splat(): embedded[:, None, :] * row_kernel[level][None]  16.6 us
    unnamed x55, local copies, waits for them, and re-layouts  13.7 us
    dot_general x4, matrix products, splat(): lax.dot_general(weighted, column_kernel[level], (((1,), (1,)), ((), ())),...  13 us
    all_to_all x1, waiting for transfers between devices, on_device(): lax.all_to_all(outgoing, 'band', split_axis=1, concat_axis=1, tiled=True)  12.5 us
    all_to_all x1, starting transfers between devices, on_device(): lax.all_to_all(outgoing, 'band', split_axis=1, concat_axis=1, tiled=True)  12.3 us
  transfers between devices with their start and end apart: 6, of which 5 were waited for; matrix products, arithmetic and copies ran while one was open for 8% of the time, Pallas kernels for 0%

profile of v1, /device:TPU:2, one launch (start us, length us, event | category | flops | bytes accessed | tf_op | source)
XLA Modules:
  0.0 400.6 jit_solution(18087226297286206863)
XLA Ops:
  14.1 2.3 scatter_fusion
  16.5 2.3 scatter_fusion.1
  21.7 12.3 %all-to-all-start = ((bf16[64,2,1050]{2,1,0:T(2,128)(2,1)}), bf16[64,2,1050]{2,1,0:T(2,128)(2,1)S(1)}, u32[]{:S(2)}, u32[]{:S(2)}) async-start(bf16[64,2,1050]{2,1,0:T(2,128)(2,1)} %reshape.419), calls=%async_computation | async-start | bytes 589824 | tf_op jit(solution)/shard_map/all_to_all | solution.py:127
  34.1 12.5 %all-to-all-done = bf16[64,2,1050]{2,1,0:T(2,128)(2,1)S(1)} async-done(((bf16[64,2,1050]{2,1,0:T(2,128)(2,1)}), bf16[64,2,1050]{2,1,0:T(2,128)(2,1)S(1)}, u32[]{:S(2)}, u32[]{:S(2)}) %all-to-all-start) | async-done | bytes 268832 | tf_op jit(solution)/shard_map/all_to_all | solution.py:127
  50.7 2.9 exponential_convert_fusion
  58.4 6.8 %broadcast_multiply_fusion.3 = (bf16[32,12,3840]{2,1,0:T(8,128)(2,1)}, bf16[32,12,3840]{2,1,0:T(8,128)(2,1)}, bf16[32,12,3840]{2,1,0:T(8,128)(2,1)}, bf16[32,12,3840]{2,1,0:T(8,128)(2,1)}) fusion(bf16[12,3840]{1,0:T(8,128)(2,1)} %get-tuple-element.34, bf16[32,3840]{1,0:T(8,128)(2,1)S(1)} %mul.298, bf16[12,3840]{1,0:T(8,128)(2,1)} %get-tuple-element.33, ...), kind=kLoop, calls=%fused_computation.37 | loop fusion | flops 5898240 | bytes 12410880 | tf_op jit(solution)/shard_map/mul | solution.py:53
  65.2 3.9 mul.315
  69.1 3.2 fusion.18
  72.3 2.1 stack.55
  74.5 3.9 mul.326
  78.4 3.3 fusion.14
  81.6 2.2 stack.56
  83.8 3.9 mul.330
  87.7 3.2 fusion.10
  93.1 4.1 %mul.334 = bf16[384,3840]{1,0:T(8,128)(2,1)S(1)} reshape(bf16[32,12,3840]{2,1,0:T(8,128)(2,1)} %get-tuple-element.38) | data formatting | bytes 5898240 | tf_op jit(solution)/shard_map/mul | solution.py:53
  97.2 3.2 fusion.6
  102.0 2.8 fusion.54
  106.0 4.8 %all-to-all-start.1 = ((bf16[128,4,768]{2,0,1:T(8,128)(2,1)}), bf16[128,4,768]{2,0,1:T(8,128)(2,1)S(1)}, u32[]{:S(2)}, u32[]{:S(2)}) async-start(bf16[128,4,768]{2,0,1:T(8,128)(2,1)} %copy.51), calls=%async_computation.1 | async-start | bytes 1572864 | tf_op jit(solution)/shard_map/all_to_all | solution.py:133
  114.0 8.0 %all-to-all-done.1 = bf16[128,4,768]{2,0,1:T(8,128)(2,1)S(1)} async-done(((bf16[128,4,768]{2,0,1:T(8,128)(2,1)}), bf16[128,4,768]{2,0,1:T(8,128)(2,1)S(1)}, u32[]{:S(2)}, u32[]{:S(2)}) %all-to-all-start.1) | async-done | bytes 786464 | tf_op jit(solution)/shard_map/all_to_all | solution.py:133
  126.1 4.9 %all-to-all-start.2 = ((bf16[4,128,768]{2,1,0:T(8,128)(2,1)}), bf16[4,128,768]{2,1,0:T(8,128)(2,1)S(1)}, u32[]{:S(2)}, u32[]{:S(2)}) async-start(bf16[4,128,768]{2,1,0:T(8,128)(2,1)} %bitcast.182), calls=%async_computation.2 | async-start | bytes 1572864 | tf_op jit(solution)/shard_map/all_to_all | solution.py:161
  131.4 2.8 fusion.90
  135.9 5.3 %all-to-all-done.2 = bf16[4,128,768]{2,1,0:T(8,128)(2,1)S(1)} async-done(((bf16[4,128,768]{2,1,0:T(8,128)(2,1)}), bf16[4,128,768]{2,1,0:T(8,128)(2,1)S(1)}, u32[]{:S(2)}, u32[]{:S(2)}) %all-to-all-start.2) | async-done | bytes 786464 | tf_op jit(solution)/shard_map/all_to_all | solution.py:161
  142.2 3.4 slice_reduce_fusion.2
  145.6 2.7 fusion.23
  148.3 2.6 fusion.20
  155.2 2.6 reshape.421
  157.8 6.2 %all-to-all-start.3 = ((f32[64,1,1920]{2,1,0:T(1,128)}), f32[64,1,1920]{2,1,0:T(1,128)S(1)}, u32[]{:S(2)}, u32[]{:S(2)}) async-start(f32[64,1,1920]{2,1,0:T(1,128)} %reshape.421), calls=%async_computation.3 | async-start | bytes 983040 | tf_op jit(solution)/shard_map/all_to_all | solution.py:164
  164.1 31.5 %all-reduce.7.cloned.1.call-done = (f32[512,512]{1,0:T(8,128)}, f32[512,512]{1,0:T(8,128)}) async-done(((f32[512,512]{1,0:T(8,128)}, f32[512,512]{1,0:T(8,128)}), (f32[512,512]{1,0:T(8,128)}, f32[512,512]{1,0:T(8,128)})) %all-reduce.7.cloned.1.call-update) | async-done | bytes 2097168 | tf_op jit(solution)/shard_map/psum | solution.py:162
  195.7 9.5 %psum.44 = f32[512]{0:T(512)S(1)} all-reduce(f32[512]{0:T(512)S(1)} %get-tuple-element.48), channel_id=1, replica_groups=mesh['band'=64,'rep'=4] {'rep'}, use_global_device_ids=true, to_apply=%region_13.14 | all-reduce | flops 512 | bytes 4096 | tf_op jit(solution)/shard_map/psum | solution.py:162
  205.1 127.5 %psum.45 = f32[512]{0:T(512)} all-reduce(f32[512]{0:T(512)S(1)} %psum.44), channel_id=1, replica_groups=mesh['band'=64,'rep'=4] {'band'}, use_global_device_ids=true, to_apply=%region_14.15 | all-reduce | flops 512 | bytes 4096 | tf_op jit(solution)/shard_map/psum | solution.py:162
  342.5 47.8 %all-reduce.5.cloned.1.call-done = (f32[512,512]{1,0:T(8,128)}, f32[512,512]{1,0:T(8,128)}) async-done(((f32[512,512]{1,0:T(8,128)}, f32[512,512]{1,0:T(8,128)}), (f32[512,512]{1,0:T(8,128)}, f32[512,512]{1,0:T(8,128)})) %all-reduce.5.cloned.1.call-update) | async-done | bytes 2097168 | tf_op jit(solution)/shard_map/psum | solution.py:162
  390.2 2.4 copy.102
  (124 shorter events, 48.7 us)
Async XLA Ops:
  7.2 114.8 %copy-start = (bf16[512,512]{1,0:T(8,128)(2,1)S(1)}, bf16[512,512]{1,0:T(8,128)(2,1)}, u32[]{:S(2)}) copy-start(bf16[512,512]{1,0:T(8,128)(2,1)} %param.12) | copy-start | bytes 1572868
  19.1 15.0 %copy-start.16 = (f32[4]{0:T(128)S(1)}, f32[4]{0:T(128)}, u32[]{:S(2)}) copy-start(f32[4]{0:T(128)} %param.11) | copy-start | bytes 52
  21.7 24.9 %all-to-all-start = ((bf16[64,2,1050]{2,1,0:T(2,128)(2,1)}), bf16[64,2,1050]{2,1,0:T(2,128)(2,1)S(1)}, u32[]{:S(2)}, u32[]{:S(2)}) async-start(bf16[64,2,1050]{2,1,0:T(2,128)(2,1)} %reshape.419), calls=%async_computation | async-start | bytes 589824 | tf_op jit(solution)/shard_map/all_to_all | solution.py:127
  48.3 0.8 copy-start.2
  53.6 3.1 copy-start.1
  53.7 1.7 copy-start.3
  105.0 5.8 %copy-start.6 = (bf16[512,3,256]{2,0,1:T(8,128)(2,1)S(1)}, bf16[512,3,256]{2,0,1:T(8,128)(2,1)}, u32[]{:S(2)}) copy-start(bf16[512,3,256]{2,0,1:T(8,128)(2,1)} %param.15) | copy-start | bytes 2359300
  106.0 15.9 %all-to-all-start.1 = ((bf16[128,4,768]{2,0,1:T(8,128)(2,1)}), bf16[128,4,768]{2,0,1:T(8,128)(2,1)S(1)}, u32[]{:S(2)}, u32[]{:S(2)}) async-start(bf16[128,4,768]{2,0,1:T(8,128)(2,1)} %copy.51), calls=%async_computation.1 | async-start | bytes 1572864 | tf_op jit(solution)/shard_map/all_to_all | solution.py:133
  112.2 9.7 %copy-start.15 = (f32[512]{0:T(512)S(1)}, f32[512]{0:T(512)}, u32[]{:S(2)}) copy-start(f32[512]{0:T(512)} %param.13) | copy-start | bytes 6148
  114.0 8.6 %copy-start.7 = (bf16[512,3,256]{0,2,1:T(8,128)(2,1)S(1)}, bf16[512,3,256]{0,2,1:T(8,128)(2,1)}, u32[]{:S(2)}) copy-start(bf16[512,3,256]{0,2,1:T(8,128)(2,1)} %copy.39) | copy-start | bytes 2359300
  114.0 8.6 %copy-start.14 = (bf16[512,512]{1,0:T(8,128)(2,1)S(1)}, bf16[512,512]{1,0:T(8,128)(2,1)}, u32[]{:S(2)}) copy-start(bf16[512,512]{1,0:T(8,128)(2,1)} %param.14) | copy-start | bytes 1572868
  122.6 1.4 copy-start.17
  122.6 2.0 copy-start.4
  123.9 2.1 copy-start.8
  126.1 15.2 %all-to-all-start.2 = ((bf16[4,128,768]{2,1,0:T(8,128)(2,1)}), bf16[4,128,768]{2,1,0:T(8,128)(2,1)S(1)}, u32[]{:S(2)}, u32[]{:S(2)}) async-start(bf16[4,128,768]{2,1,0:T(8,128)(2,1)} %bitcast.182), calls=%async_computation.2 | async-start | bytes 1572864 | tf_op jit(solution)/shard_map/all_to_all | solution.py:161
  131.0 64.6 %all-reduce.7.cloned.1.call-start = ((), (), s32[]{:S(2)}) async-start(), calls=%async_computation.5 | async-start | bytes 4194304 | tf_op jit(solution)/shard_map/psum | solution.py:162
  131.4 2.8 copy-start.18
  141.8 3.7 copy-start.12
  142.1 8.8 %slice-start = ((s8[7864320]{0:T(1024)(128)(4,1)}), s8[3670016]{0:T(1024)(128)(4,1)S(1)}, s32[]{:S(2)}) async-start(s8[7864320]{0:T(1024)(128)(4,1)} %bitcast.170), calls=%async_computation.6 | async-start | bytes 7340032
  145.6 2.7 copy-start.11
  145.6 5.3 %slice-start.1 = ((s8[7864320]{0:T(1024)(128)(4,1)}), s8[4194304]{0:T(1024)(128)(4,1)S(1)}, s32[]{:S(2)}) async-start(s8[7864320]{0:T(1024)(128)(4,1)} %bitcast.170), calls=%async_computation.7 | async-start | bytes 8388608
  148.3 2.6 copy-start.10
  150.9 1.0 copy-start.9
  155.2 40.5 %copy-start.13 = (s32[512,1]{0,1:T(1,128)S(1)}, s32[512,1]{0,1:T(1,128)}, u32[]{:S(2)}) copy-start(s32[512,1]{0,1:T(1,128)} %param.9) | copy-start | bytes 6148
  157.8 174.8 %all-to-all-start.3 = ((f32[64,1,1920]{2,1,0:T(1,128)}), f32[64,1,1920]{2,1,0:T(1,128)S(1)}, u32[]{:S(2)}, u32[]{:S(2)}) async-start(f32[64,1,1920]{2,1,0:T(1,128)} %reshape.421), calls=%async_computation.3 | async-start | bytes 983040 | tf_op jit(solution)/shard_map/all_to_all | solution.py:164
  164.0 226.2 %all-reduce.5.cloned.1.call-start = ((), (), s32[]{:S(2)}) async-start(), calls=%async_computation.4 | async-start | bytes 4194304 | tf_op jit(solution)/shard_map/psum | solution.py:162
  390.2 2.4 copy-start.5
Sparse Core Ops, SparseCore 0:
  136.0 59.5 all-reduce.6
  199.5 190.6 all-reduce.4
